TPU v7x, 32 devices: a whole 2x2x4 slice. The times are simulated.
32 devices in a mesh: groups: 2 (over x), expert: 16 (over z, y, core).
Axes of the slice: x: 2, y: 2, z: 4, core: 2. Of those that a mesh axis runs over, the one named last changes fastest.
Arguments:
- tokens: bfloat16 [512, 2048], P(('groups', 'expert')), parts along dimension 0, may hold values from -6 to 6
- tangent: bfloat16 [512, 2048], P(('groups', 'expert')), parts along dimension 0, may hold values from -6 to 6
- cotangent: bfloat16 [512, 2048], P(('groups', 'expert')), parts along dimension 0, may hold values from -6 to 6
- routes: int32 [512, 8], P(('groups', 'expert')), parts along dimension 0, may hold values from 0 to 15, as said below
- route_weight: bfloat16 [512, 8], P(('groups', 'expert')), parts along dimension 0, may hold values from 0.099609375 to 1
- gate_weight: bfloat16 [16, 2048, 768], P('expert'), may hold values from -0.125 to 0.125
- up_weight: bfloat16 [16, 2048, 768], P('expert'), may hold values from -0.125 to 0.125
- down_weight: bfloat16 [16, 768, 2048], P('expert'), may hold values from -0.21875 to 0.21875
Outputs:
- hvp: float32 [512, 2048], P(('groups', 'expert')), parts along dimension 0
There are 2 independent parts, one for each index of `groups`. A program takes and returns all parts, laid end to end along the dimension named above; an argument that names none is the same for every part. Nothing has to cross between parts.
Inputs may be any that keep to these rules, and one draw needn't show every extreme that they name: `routes`: each row names 8 different experts. Among the rows of one device no expert is named more than 16 times, and one expert is named exactly 16 times among the rows of every device.
All inputs are finite; a program needn't handle non-finite values.
Results may differ from a plain program's by a relative error of at most 0.004.
Values may be sent and summed in bfloat16 or wider, within the bound.
A program may use at most 64 MiB of HBM per device.

v0:
```python
import jax
import jax.numpy as jnp
from jax import lax
from jax.sharding import PartitionSpec as P


def route_terms(rows_x, rows_v, rows_c, rows_w, gate_w, up_w, down_w):
    count = rows_x.shape[0]
    stacked = jnp.concatenate([rows_x, rows_v], axis=0)
    gate_both = jnp.dot(stacked, gate_w, preferred_element_type=jnp.float32)
    up_both = jnp.dot(stacked, up_w, preferred_element_type=jnp.float32)
    gate = gate_both[:count]
    gate_dot = gate_both[count:]
    upper = up_both[:count]
    up_dot = up_both[count:]
    back = lax.dot_general(
        rows_c, down_w, (((1,), (1,)), ((), ())), preferred_element_type=jnp.float32
    )
    back = back * rows_w.astype(jnp.float32)[:, None]
    sigma = jax.nn.sigmoid(gate)
    first = sigma * (1.0 + gate * (1.0 - sigma))
    second = sigma * (1.0 - sigma) * (2.0 + gate * (1.0 - 2.0 * sigma))
    gate_change = (back * (up_dot * first + upper * second * gate_dot)).astype(jnp.bfloat16)
    up_change = (back * first * gate_dot).astype(jnp.bfloat16)
    term = lax.dot_general(
        gate_change, gate_w, (((1,), (1,)), ((), ())), preferred_element_type=jnp.float32
    )
    term = term + lax.dot_general(
        up_change, up_w, (((1,), (1,)), ((), ())), preferred_element_type=jnp.float32
    )
    return term.astype(jnp.bfloat16)


def shards(tokens, tangent, cotangent, routes, route_weight, gate_weight, up_weight, down_weight):
    experts = lax.axis_size("expert")
    tok_rows, width = tokens.shape
    top_count = routes.shape[1]
    slots = 2 * tok_rows * top_count // experts
    routed = tok_rows * top_count
    flat_routes = routes.reshape(-1)
    onehot = (flat_routes[:, None] == jnp.arange(experts, dtype=jnp.int32)[None, :]).astype(
        jnp.int32
    )
    slot_rank = jnp.sum((jnp.cumsum(onehot, axis=0) - onehot) * onehot, axis=1)
    target = flat_routes * slots + slot_rank
    source = (
        jnp.zeros((experts * slots,), jnp.int32).at[target].set(jnp.arange(routed, dtype=jnp.int32))
    )
    filled = jnp.zeros((experts * slots,), jnp.bool_).at[target].set(True)
    owner = source // top_count

    def place(values):
        picked = jnp.where(filled[:, None], values[owner], jnp.zeros((), values.dtype))
        return picked.reshape(experts, slots, width)

    send_x = place(tokens)
    send_v = place(tangent)
    send_c = place(cotangent)
    send_w = jnp.where(
        filled, route_weight.reshape(-1)[source], jnp.zeros((), route_weight.dtype)
    ).reshape(experts, slots)
    gate_w = gate_weight[0]
    up_w = up_weight[0]
    down_w = down_weight[0]
    recv_w = lax.all_to_all(send_w, "expert", split_axis=0, concat_axis=0, tiled=True)
    sources, levels = recv_w.shape
    result = route_terms(
        lax.all_to_all(send_x, "expert", split_axis=0, concat_axis=0, tiled=True).reshape(
            -1, width
        ),
        lax.all_to_all(send_v, "expert", split_axis=0, concat_axis=0, tiled=True).reshape(
            -1, width
        ),
        lax.all_to_all(send_c, "expert", split_axis=0, concat_axis=0, tiled=True).reshape(
            -1, width
        ),
        recv_w.reshape(-1),
        gate_w,
        up_w,
        down_w,
    )
    terms = result.reshape(sources, levels, width)
    returned = lax.all_to_all(terms, "expert", split_axis=0, concat_axis=0, tiled=True)
    back_flat = returned.reshape(experts * slots, width)
    per_route = back_flat[target].astype(jnp.float32).reshape(tok_rows, top_count, width)
    return jnp.sum(per_route, axis=1)


def solution(mesh):
    placed = (
        P(("groups", "expert"), None),
        P(("groups", "expert"), None),
        P(("groups", "expert"), None),
        P(("groups", "expert"), None),
        P(("groups", "expert"), None),
        P("expert", None, None),
        P("expert", None, None),
        P("expert", None, None),
    )
    return jax.shard_map(
        shards, mesh=mesh, in_specs=placed, out_specs=P(("groups", "expert"), None), check_vma=False
    )
```

profile of v0, /device:TPU:0, one launch (start us, length us, event | category | flops | bytes accessed | tf_op | source)
XLA Modules:
  0.0 158.1 jit_solution(14118444045055718604)
XLA Ops:
  0.0 0.8 broadcast_multiply_fusion
  0.9 0.9 copy.16
  1.8 0.8 copy.17
  2.5 0.1 reshape.86
  2.7 0.1 mul.65
  2.8 0.1 eq.15
  2.9 0.1 fusion.30
  3.0 0.2 reduce_window_sum.11
  3.1 0.2 select_reduce_fusion
  3.3 1.0 scatter_custom_fusion.1
  4.3 1.0 scatter_custom_fusion
  5.4 1.9 %gather_fusion.1 = bf16[256]{0:T(256)(128)(2,1)S(1)} fusion(bf16[128]{0:T(256)(128)(2,1)S(1)} %reshape.86, s32[1024]{0:T(1024)S(1)} %get-tuple-element.10), kind=kCustom, calls=%fused_computation.1 | custom fusion | bytes 2048 | tf_op jit(solution)/shard_map/gather | solution.py:60
  7.3 0.7 all_to_all.24
  8.0 7.4 %all-to-all-start.1 = ((bf16[16,1,16]{2,1,0:T(2,128)(2,1)}), bf16[16,1,16]{2,1,0:T(2,128)(2,1)S(1)}, u32[]{:S(2)}, u32[]{:S(2)}) async-start(bf16[16,1,16]{2,1,0:T(2,128)(2,1)} %all_to_all.24), calls=%async_computation.1 | async-start | bytes 16384 | tf_op jit(solution)/shard_map/all_to_all | solution.py:65
  15.4 2.3 %gather_fusion.3 = bf16[256,2048]{1,0:T(8,128)(2,1)} fusion(bf16[16,2048]{1,0:T(8,128)(2,1)S(1)} %copy-done.1, s32[1024]{0:T(1024)S(1)} %get-tuple-element.11), kind=kCustom, calls=%fused_computation.3 | custom fusion | bytes 2098176 | tf_op jit(solution)/shard_map/gather | solution.py:53
  17.8 2.4 %gather_fusion.2 = bf16[256,2048]{1,0:T(8,128)(2,1)} fusion(bf16[16,2048]{1,0:T(8,128)(2,1)S(1)} %copy-done.2, s32[1024]{0:T(1024)S(1)} %get-tuple-element.11), kind=kCustom, calls=%fused_computation.2 | custom fusion | bytes 2098176 | tf_op jit(solution)/shard_map/gather | solution.py:53
  20.1 2.4 %gather_fusion = bf16[256,2048]{1,0:T(8,128)(2,1)} fusion(bf16[16,2048]{1,0:T(8,128)(2,1)S(1)} %copy-done.3, s32[1024]{0:T(1024)S(1)} %get-tuple-element.11), kind=kCustom, calls=%fused_computation | custom fusion | bytes 2098176 | tf_op jit(solution)/shard_map/gather | solution.py:53
  22.5 3.6 %broadcast_select_fusion.1 = (bf16[16,16,2048]{2,1,0:T(8,128)(2,1)}, bf16[16,16,2048]{2,1,0:T(8,128)(2,1)}, bf16[16,16,2048]{2,1,0:T(8,128)(2,1)}) fusion(bf16[16,16,2048]{2,1,0:T(8,128)(2,1)} %bitcast.40, pred[16,16]{1,0:T(8,128)(4,1)S(1)} %broadcast_in_dim.50, bf16[16,16,2048]{2,1,0:T(8,128)(2,1)} %bitcast.39, bf16[16,16,2048]{2,1,0:T(8,128)(2,1)} %bitcast.41), kind=kLoop, calls=%fused_computation.25 | loop fusion | flops 1572864 | bytes 6291712 | tf_op jit(solution)/shard_map/jit(_where)/select_n | solution.py:53
  26.1 31.0 %all_to_all.30 = bf16[16,16,2048]{2,1,0:T(8,128)(2,1)} all-to-all(bf16[16,16,2048]{2,1,0:T(8,128)(2,1)} %get-tuple-element.5), channel_id=1, replica_groups=mesh['groups'=2,'expert'=16] {'expert'}, dimensions={0} | all-to-all | bytes 2097152 | tf_op jit(solution)/shard_map/all_to_all | solution.py:68
  57.1 29.9 %all_to_all.31 = bf16[16,16,2048]{2,1,0:T(8,128)(2,1)} all-to-all(bf16[16,16,2048]{2,1,0:T(8,128)(2,1)} %get-tuple-element.6), channel_id=1, replica_groups=mesh['groups'=2,'expert'=16] {'expert'}, dimensions={0} | all-to-all | bytes 2097152 | tf_op jit(solution)/shard_map/all_to_all | solution.py:71
  87.0 5.0 %all-to-all-start = ((bf16[16,16,2048]{2,1,0:T(8,128)(2,1)}), bf16[16,16,2048]{2,1,0:T(8,128)(2,1)}, u32[]{:S(2)}, u32[]{:S(2)}) async-start(bf16[16,16,2048]{2,1,0:T(8,128)(2,1)} %get-tuple-element.7), calls=%async_computation | async-start | bytes 2097152 | tf_op jit(solution)/shard_map/all_to_all | solution.py:74
  92.2 4.6 %fusion.2 = f32[512,768]{1,0:T(8,128)} fusion(bf16[1,2048,768]{2,1,0:T(8,128)(2,1)S(1)} %copy-done, bf16[256,2048]{1,0:T(8,128)(2,1)} %bitcast.44, bf16[256,2048]{1,0:T(8,128)(2,1)} %bitcast.42), kind=kOutput, calls=%fused_computation.9 | convolution fusion | flops 1614807040 | bytes 6815744 | tf_op jit(solution)/shard_map/dot_general | solution.py:10
  96.9 3.0 %fusion.6 = f32[512,768]{1,0:T(8,128)} fusion(bf16[1,2048,768]{2,1,0:T(8,128)(2,1)S(1)} %copy-done.6, bf16[256,2048]{1,0:T(8,128)(2,1)S(1)} %bitcast.45, bf16[256,2048]{1,0:T(8,128)(2,1)S(1)} %bitcast.43), kind=kOutput, calls=%fused_computation.13 | convolution fusion | flops 1614807040 | bytes 6815744 | tf_op jit(solution)/shard_map/dot_general | solution.py:11
  99.8 15.2 %all-to-all-done = bf16[16,16,2048]{2,1,0:T(8,128)(2,1)} async-done(((bf16[16,16,2048]{2,1,0:T(8,128)(2,1)}), bf16[16,16,2048]{2,1,0:T(8,128)(2,1)}, u32[]{:S(2)}, u32[]{:S(2)}) %all-to-all-start) | async-done | bytes 1048608 | tf_op jit(solution)/shard_map/all_to_all | solution.py:74
  115.1 3.4 %fusion.16 = f32[256,768]{1,0:T(8,128)S(1)} fusion(bf16[256,2048]{1,0:T(8,128)(2,1)} %bitcast.3, bf16[1,768,2048]{2,1,0:T(8,128)(2,1)} %param.15, f32[256]{0:T(256)S(1)} %reshape.91), kind=kOutput, calls=%fused_computation.20 | convolution fusion | flops 805502976 | bytes 4981760 | tf_op jit(solution)/shard_map/dot_general | solution.py:16
  118.5 1.5 fusion
  120.0 0.4 copy-done.7
  120.4 2.1 %fusion.13 = bf16[256,2048]{1,0:T(8,128)(2,1)} fusion(f32[256,2048]{1,0:T(8,128)S(1)} %fusion, bf16[1,2048,768]{2,1,0:T(8,128)(2,1)S(1)} %copy-done.7, f32[256,768]{1,0:T(8,128)S(1)} %fusion.16, f32[512,768]{1,0:T(8,128)S(1)} %copy-done.8), kind=kOutput, calls=%fused_computation.18 | convolution fusion | flops 808321024 | bytes 8650752 | tf_op jit(solution)/shard_map/dot_general | solution.py:28
  122.5 6.9 %all-to-all-start.4 = ((bf16[16,16,2048]{2,1,0:T(8,128)(2,1)}), bf16[16,16,2048]{2,1,0:T(8,128)(2,1)}, u32[]{:S(2)}, u32[]{:S(2)}) async-start(bf16[16,16,2048]{2,1,0:T(8,128)(2,1)} %bitcast.46), calls=%async_computation.4 | async-start | bytes 2097152 | tf_op jit(solution)/shard_map/all_to_all | solution.py:83
  129.4 23.0 %all-to-all-done.4 = bf16[16,16,2048]{2,1,0:T(8,128)(2,1)} async-done(((bf16[16,16,2048]{2,1,0:T(8,128)(2,1)}), bf16[16,16,2048]{2,1,0:T(8,128)(2,1)}, u32[]{:S(2)}, u32[]{:S(2)}) %all-to-all-start.4) | async-done | bytes 1048608 | tf_op jit(solution)/shard_map/all_to_all | solution.py:83
  152.4 3.6 %gather_fusion.4 = bf16[128,2048]{1,0:T(8,128)(2,1)} fusion(bf16[256,2048]{1,0:T(8,128)(2,1)} %bitcast.12, s32[1024]{0:T(1024)S(1)} %pad_clamp_fusion), kind=kCustom, calls=%fused_computation.4 | custom fusion | bytes 1049088 | tf_op jit(solution)/shard_map/gather | solution.py:85
  156.0 2.0 %convert_reduce_fusion = f32[16,2048]{1,0:T(8,128)} fusion(bf16[128,2048]{1,0:T(8,128)(2,1)} %gather_fusion.4), kind=kLoop, calls=%fused_computation.23 | loop fusion | flops 491520 | bytes 655360 | tf_op jit(solution)/shard_map/reduce_sum | solution.py:86
  (31 shorter events, 0.4 us)
Async XLA Ops:
  0.0 92.2 %copy-start = (bf16[1,2048,768]{2,1,0:T(8,128)(2,1)S(1)}, bf16[1,2048,768]{2,1,0:T(8,128)(2,1)}, u32[]{:S(2)}) copy-start(bf16[1,2048,768]{2,1,0:T(8,128)(2,1)} %param.13) | copy-start | bytes 9437188
  0.0 15.4 %copy-start.1 = (bf16[16,2048]{1,0:T(8,128)(2,1)S(1)}, bf16[16,2048]{1,0:T(8,128)(2,1)}, u32[]{:S(2)}) copy-start(bf16[16,2048]{1,0:T(8,128)(2,1)} %param.9) | copy-start | bytes 196612
  8.0 18.2 %all-to-all-start.1 = ((bf16[16,1,16]{2,1,0:T(2,128)(2,1)}), bf16[16,1,16]{2,1,0:T(2,128)(2,1)S(1)}, u32[]{:S(2)}, u32[]{:S(2)}) async-start(bf16[16,1,16]{2,1,0:T(2,128)(2,1)} %all_to_all.24), calls=%async_computation.1 | async-start | bytes 16384 | tf_op jit(solution)/shard_map/all_to_all | solution.py:65
  15.4 2.3 %copy-start.2 = (bf16[16,2048]{1,0:T(8,128)(2,1)S(1)}, bf16[16,2048]{1,0:T(8,128)(2,1)}, u32[]{:S(2)}) copy-start(bf16[16,2048]{1,0:T(8,128)(2,1)} %param.8) | copy-start | bytes 196612
  17.8 2.4 %copy-start.3 = (bf16[16,2048]{1,0:T(8,128)(2,1)S(1)}, bf16[16,2048]{1,0:T(8,128)(2,1)}, u32[]{:S(2)}) copy-start(bf16[16,2048]{1,0:T(8,128)(2,1)} %param.10) | copy-start | bytes 196612
  87.0 28.0 %all-to-all-start = ((bf16[16,16,2048]{2,1,0:T(8,128)(2,1)}), bf16[16,16,2048]{2,1,0:T(8,128)(2,1)}, u32[]{:S(2)}, u32[]{:S(2)}) async-start(bf16[16,16,2048]{2,1,0:T(8,128)(2,1)} %get-tuple-element.7), calls=%async_computation | async-start | bytes 2097152 | tf_op jit(solution)/shard_map/all_to_all | solution.py:74
  92.2 4.7 %copy-start.4 = (bf16[16,16,2048]{2,1,0:T(8,128)(2,1)S(1)}, bf16[16,16,2048]{2,1,0:T(8,128)(2,1)}, u32[]{:S(2)}) copy-start(bf16[16,16,2048]{2,1,0:T(8,128)(2,1)} %all_to_all.30) | copy-start | bytes 3145732
  92.2 4.7 %copy-start.5 = (bf16[16,16,2048]{2,1,0:T(8,128)(2,1)S(1)}, bf16[16,16,2048]{2,1,0:T(8,128)(2,1)}, u32[]{:S(2)}) copy-start(bf16[16,16,2048]{2,1,0:T(8,128)(2,1)} %all_to_all.31) | copy-start | bytes 3145732
  92.2 4.7 %copy-start.6 = (bf16[1,2048,768]{2,1,0:T(8,128)(2,1)S(1)}, bf16[1,2048,768]{2,1,0:T(8,128)(2,1)}, u32[]{:S(2)}) copy-start(bf16[1,2048,768]{2,1,0:T(8,128)(2,1)} %param.14) | copy-start | bytes 9437188
  115.1 3.4 %copy-start.8 = (f32[512,768]{1,0:T(8,128)S(1)}, f32[512,768]{1,0:T(8,128)}, u32[]{:S(2)}) copy-start(f32[512,768]{1,0:T(8,128)} %fusion.2) | copy-start | bytes 4718596
  115.1 3.4 %copy-start.9 = (f32[512,768]{1,0:T(8,128)S(1)}, f32[512,768]{1,0:T(8,128)}, u32[]{:S(2)}) copy-start(f32[512,768]{1,0:T(8,128)} %fusion.6) | copy-start | bytes 4718596
  118.5 1.9 %copy-start.7 = (bf16[1,2048,768]{2,1,0:T(8,128)(2,1)S(1)}, bf16[1,2048,768]{2,1,0:T(8,128)(2,1)}, u32[]{:S(2)}) copy-start(bf16[1,2048,768]{2,1,0:T(8,128)(2,1)} %param.14) | copy-start | bytes 9437188
  122.5 29.9 %all-to-all-start.4 = ((bf16[16,16,2048]{2,1,0:T(8,128)(2,1)}), bf16[16,16,2048]{2,1,0:T(8,128)(2,1)}, u32[]{:S(2)}, u32[]{:S(2)}) async-start(bf16[16,16,2048]{2,1,0:T(8,128)(2,1)} %bitcast.46), calls=%async_computation.4 | async-start | bytes 2097152 | tf_op jit(solution)/shard_map/all_to_all | solution.py:83
where the time goes:
time: 160 us; the launch traced here: 158 us
  blocking collectives  60.9 us (38%)
  waiting for transfers between devices  38.2 us (24%)
  starting transfers between devices  19.3 us (12%)
  local copies, waits for them, and re-layouts  17.8 us (11%)
  matrix products  14.6 us (9%)
  other arithmetic  7.01 us (4%)
    all_to_all x1, blocking collectives, shards(): lax.all_to_all(send_x, 'expert', split_axis=0, concat_axis=0, tiled=True)  31 us
    all_to_all x1, blocking collectives, shards(): lax.all_to_all(send_v, 'expert', split_axis=0, concat_axis=0, tiled=True)  29.9 us
    all_to_all x1, waiting for transfers between devices, shards(): lax.all_to_all(terms, 'expert', split_axis=0, concat_axis=0, tiled=True)  23 us
    all_to_all x1, waiting for transfers between devices, shards(): lax.all_to_all(send_c, 'expert', split_axis=0, concat_axis=0, tiled=True)  15.2 us
    all_to_all x1, starting transfers between devices, shards(): lax.all_to_all(send_w, 'expert', split_axis=0, concat_axis=0, tiled=True)  7.39 us
    gather x3, local copies, waits for them, and re-layouts, place(): values[owner]  7.04 us
    all_to_all x1, starting transfers between devices, shards(): lax.all_to_all(terms, 'expert', split_axis=0, concat_axis=0, tiled=True)  6.9 us
    all_to_all x1, starting transfers between devices, shards(): lax.all_to_all(send_c, 'expert', split_axis=0, concat_axis=0, tiled=True)  5.04 us
  transfers between devices with their start and end apart: 3, of which 2 were waited for; matrix products, arithmetic and copies ran while one was open for 12% of the time, Pallas kernels for 0%

commit v1 on v0

--- a/solution.py
+++ b/solution.py
@@ -1,7 +1,363 @@
+import functools
+
 import jax
 import jax.numpy as jnp
 from jax import lax
+from jax.experimental import pallas as pl
+from jax.experimental.pallas import tpu as pltpu
 from jax.sharding import PartitionSpec as P
+
+LANES = 128
+BF16 = jnp.bfloat16
+F32 = jnp.float32
+NT = (((1,), (1,)), ((), ()))
+
+
+def whole_block_kernel(
+    lines, parts,
+    x_hbm, v_hbm, c_hbm, routes_ref, rw_ref, g_hbm, u_hbm, d_hbm, out_ref,
+    xv, cw, g, u, d, a_s, b_s, gc, uc, term, q,
+    s1, r1, s2, r2, su, ru, sd, rd,
+    local, zs, zr, ys, yr, ss, sr, rs_s, rs_r, us, ur, ds_, dr,
+):
+    rows, width = x_hbm.shape
+    hidden = g.shape[1]
+    total = lines * 4 * rows
+    piece = width // parts
+    me = lax.axis_index("expert")
+    core = lax.rem(me, 2)
+    y = lax.rem(lax.div(me, 2), 2)
+    z = lax.div(me, 4)
+    last = lines - 1
+
+    def dev(zz, yy, cc):
+        return (zz * 2 + yy) * 2 + cc
+
+    sib = dev(z, y, 1 - core)
+    ynb = dev(z, 1 - y, core)
+
+    def remote(src, dst, send, recv, target):
+        return pltpu.make_async_remote_copy(
+            src_ref=src, dst_ref=dst, send_sem=send, recv_sem=recv,
+            device_id={"expert": target}, device_id_type=pl.DeviceIdType.MESH,
+        )
+
+    loads = [
+        pltpu.make_async_copy(x_hbm, xv.at[0, me], local.at[0]),
+        pltpu.make_async_copy(v_hbm, xv.at[1, me], local.at[1]),
+        pltpu.make_async_copy(c_hbm, cw.at[me, :, pl.ds(0, width)], local.at[2]),
+        pltpu.make_async_copy(g_hbm.at[0], g, local.at[3]),
+        pltpu.make_async_copy(u_hbm.at[0], u, local.at[4]),
+        pltpu.make_async_copy(d_hbm.at[0], d, local.at[5]),
+    ]
+    for load in loads:
+        load.start()
+
+    barrier = pltpu.get_barrier_semaphore()
+
+    def greet(target):
+        pl.semaphore_signal(
+            barrier, inc=1, device_id={"expert": target}, device_id_type=pl.DeviceIdType.MESH
+        )
+
+    greet(sib)
+    greet(ynb)
+
+    @pl.when(z > 0)
+    def _():
+        greet(me - 4)
+
+    @pl.when(z < last)
+    def _():
+        greet(me + 4)
+
+    lane = lax.broadcasted_iota(jnp.int32, (rows, LANES), 1)
+    routes = routes_ref[...]
+    weights = rw_ref[...].astype(F32)
+    table = jnp.zeros((rows, LANES), F32)
+    for k in range(routes.shape[1]):
+        table = table + jnp.where(routes[:, k : k + 1] == lane, weights[:, k : k + 1], 0.0)
+    cw[me, :, width:] = table.astype(BF16)
+
+    pl.semaphore_wait(barrier, 2 + (z > 0).astype(jnp.int32) + (z < last).astype(jnp.int32))
+
+    def block(p, index):
+        return xv.at[:, index] if p == 0 else cw.at[index]
+
+    def zcopy(p, way, s):
+        ref = block(p, dev(s, y, core))
+        return remote(ref, ref, zs.at[p, way, s], zr.at[p, way, s], me + 4 if way == 0 else me - 4)
+
+    def ycopy(p, s, col):
+        ref = block(p, dev(s, col, core))
+        return remote(ref, ref, ys.at[p, s], yr.at[p, s], ynb)
+
+    def scopy(p, k, plane):
+        ref = block(p, k * 2 + plane)
+        return remote(ref, ref, ss.at[p, k], sr.at[p, k], sib)
+
+    def pass_on(p, s, ways):
+        for way in ways:
+            @pl.when(z < last if way == 0 else z > 0)
+            def _():
+                zcopy(p, way, s).start()
+        ycopy(p, s, y).start()
+        scopy(p, s * 2 + y, core).start()
+
+    def near(t, fn):
+        @pl.when(z >= t)
+        def _():
+            fn(0, z - t)
+
+        @pl.when(z + t <= last)
+        def _():
+            fn(1, z + t)
+
+    def hop(p, t):
+        def arrive(way, s):
+            zcopy(p, way, s).wait_recv()
+            pass_on(p, s, (way,))
+        near(t, arrive)
+
+    def across(p, t):
+        def arrive(way, s):
+            ycopy(p, s, 1 - y).wait_recv()
+            scopy(p, s * 2 + 1 - y, core).start()
+        if t == 0:
+            arrive(0, z)
+        else:
+            near(t, arrive)
+
+    def from_sibling(p):
+        for k in range(lines * 2):
+            scopy(p, k, 1 - core).wait_recv()
+
+    loads[0].wait()
+    loads[1].wait()
+    pass_on(0, z, (0, 1))
+    loads[2].wait()
+    for t in range(1, lines):
+        hop(0, t)
+        across(0, t - 1)
+        if t == max(lines - 2, 1):
+            pass_on(1, z, (0, 1))
+    across(0, last)
+    loads[3].wait()
+    loads[4].wait()
+    from_sibling(0)
+
+    tile = 256
+    tiles = hidden // tile
+    both = 2 * total
+    for n in range(tiles):
+        cols = slice(n * tile, (n + 1) * tile)
+        stacked = xv[...].reshape(both, width)
+        gate_both = jnp.dot(stacked, g[:, cols], preferred_element_type=F32)
+        up_both = jnp.dot(stacked, u[:, cols], preferred_element_type=F32)
+        gate, gate_dot = gate_both[:total], gate_both[total:]
+        upper, up_dot = up_both[:total], up_both[total:]
+        sigma = jax.nn.sigmoid(gate)
+        first = sigma * (1.0 + gate * (1.0 - sigma))
+        second = sigma * (1.0 - sigma) * (2.0 + gate * (1.0 - 2.0 * sigma))
+        a_s[:, cols] = up_dot * first + upper * second * gate_dot
+        b_s[:, cols] = first * gate_dot
+        if n + 1 < lines:
+            hop(1, n + 1)
+            across(1, n)
+    for t in range(tiles + 1, lines):
+        hop(1, t)
+        across(1, t - 1)
+    for t in range(min(tiles, last), lines):
+        across(1, t)
+    loads[5].wait()
+    from_sibling(1)
+
+    tags = cw[:, :, width:].reshape(total, LANES).astype(F32)
+    mine = lax.broadcasted_iota(jnp.int32, (total, LANES), 1) == me
+    scale = jnp.sum(jnp.where(mine, tags, 0.0), axis=1, keepdims=True)
+    for n in range(tiles):
+        cols = slice(n * tile, (n + 1) * tile)
+        back = lax.dot_general(
+            cw[:, :, :width].reshape(total, width), d[cols, :], NT, preferred_element_type=F32
+        )
+        back = back * scale
+        gc[:, cols] = (back * a_s[:, cols]).astype(BF16)
+        uc[:, cols] = (back * b_s[:, cols]).astype(BF16)
+
+    def to_sibling(j):
+        return remote(s1.at[j], r1.at[j], rs_s.at[0, j], rs_r.at[0, j], sib)
+
+    def to_column(j):
+        return remote(s2.at[j], r2.at[j], rs_s.at[1, j], rs_r.at[1, j], ynb)
+
+    def up_copy(j, zd):
+        return remote(su.at[j, zd], ru.at[j, zd], us.at[j, zd], ur.at[j, zd], me + 4)
+
+    def down_copy(j, zd):
+        return remote(sd.at[j, zd], rd.at[j, zd], ds_.at[j, zd], dr.at[j, zd], me - 4)
+
+    def make_terms(j):
+        cols = slice(j * piece, (j + 1) * piece)
+        t = lax.dot_general(gc[...], g[cols, :], NT, preferred_element_type=F32)
+        t = t + lax.dot_general(uc[...], u[cols, :], NT, preferred_element_type=F32)
+        term[j] = t.reshape(lines * 4, rows, piece)
+        for k in range(lines * 2):
+            s1[j, k] = term[j, 2 * k + 1 - core].astype(BF16)
+        to_sibling(j).start()
+
+    def add_sibling(j):
+        to_sibling(j).wait_recv()
+        for zz in range(lines):
+            s2[j, zz] = (
+                term[j, dev(zz, 1 - y, core)] + r1[j, zz * 2 + 1 - y].astype(F32)
+            ).astype(BF16)
+        to_column(j).start()
+        for zz in range(lines):
+            q[j, zz] = term[j, dev(zz, y, core)] + r1[j, zz * 2 + y].astype(F32)
+
+    def add_column(j):
+        to_column(j).wait_recv()
+        for zz in range(lines):
+            q[j, zz] = q[j, zz] + r2[j, zz].astype(F32)
+
+    def wave(w, j):
+        @pl.when(z == w)
+        def _():
+            for zd in range(last, w, -1):
+                total_up = q[j, zd]
+                if w > 0:
+                    up_copy(j, zd).wait_recv()
+                    total_up = total_up + ru[j, zd].astype(F32)
+                su[j, zd] = total_up.astype(BF16)
+                up_copy(j, zd).start()
+
+        @pl.when(z == last - w)
+        def _():
+            for zd in range(0, last - w):
+                total_down = q[j, zd]
+                if w > 0:
+                    down_copy(j, zd).wait_recv()
+                    total_down = total_down + rd[j, zd].astype(F32)
+                sd[j, zd] = total_down.astype(BF16)
+                down_copy(j, zd).start()
+
+    for j in range(parts):
+        make_terms(j)
+        if j > 0:
+            add_sibling(j - 1)
+        if j > 1:
+            add_column(j - 2)
+            wave(0, j - 2)
+    add_sibling(parts - 1)
+    for j in range(max(parts - 2, 0), parts):
+        add_column(j)
+        wave(0, j)
+    for w in range(1, last):
+        for j in range(parts):
+            wave(w, j)
+    for j in range(parts):
+        cols = slice(j * piece, (j + 1) * piece)
+        out_ref[:, cols] = q[j, z]
+
+        @pl.when(z > 0)
+        def _():
+            up_copy(j, z).wait_recv()
+            out_ref[:, cols] += ru[j, z].astype(F32)
+
+        @pl.when(z < last)
+        def _():
+            down_copy(j, z).wait_recv()
+            out_ref[:, cols] += rd[j, z].astype(F32)
+
+    for p in range(2):
+        for way in (0, 1):
+            @pl.when(z < last if way == 0 else z > 0)
+            def _():
+                zcopy(p, way, z).wait_send()
+        ycopy(p, z, y).wait_send()
+        scopy(p, z * 2 + y, core).wait_send()
+        scopy(p, z * 2 + 1 - y, core).wait_send()
+        for t in range(1, lines):
+            def gone(way, s):
+                @pl.when(z < last if way == 0 else z > 0)
+                def _():
+                    zcopy(p, way, s).wait_send()
+                ycopy(p, s, y).wait_send()
+                scopy(p, s * 2 + y, core).wait_send()
+                scopy(p, s * 2 + 1 - y, core).wait_send()
+            near(t, gone)
+    for j in range(parts):
+        to_sibling(j).wait_send()
+        to_column(j).wait_send()
+        for zd in range(lines):
+            @pl.when(z < zd)
+            def _():
+                up_copy(j, zd).wait_send()
+
+            @pl.when(z > zd)
+            def _():
+                down_copy(j, zd).wait_send()
+
+
+def whole_blocks(x, v, c, routes, rw, g, u, d):
+    rows, width = x.shape
+    hidden = g.shape[2]
+    lines = lax.axis_size("expert") // 4
+    blocks = lines * 4
+    total = blocks * rows
+    parts = 4
+    piece = width // parts
+    dma = pltpu.SemaphoreType.DMA
+    anywhere = pl.BlockSpec(memory_space=pl.ANY)
+    vmem = pl.BlockSpec(memory_space=pltpu.VMEM)
+    return pl.pallas_call(
+        functools.partial(whole_block_kernel, lines, parts),
+        out_shape=jax.ShapeDtypeStruct((rows, width), F32),
+        in_specs=[anywhere] * 3 + [vmem] * 2 + [anywhere] * 3,
+        out_specs=vmem,
+        scratch_shapes=[
+            pltpu.VMEM((2, blocks, rows, width), BF16),
+            pltpu.VMEM((blocks, rows, width + LANES), BF16),
+            pltpu.VMEM((width, hidden), BF16),
+            pltpu.VMEM((width, hidden), BF16),
+            pltpu.VMEM((hidden, width), BF16),
+            pltpu.VMEM((total, hidden), F32),
+            pltpu.VMEM((total, hidden), F32),
+            pltpu.VMEM((total, hidden), BF16),
+            pltpu.VMEM((total, hidden), BF16),
+            pltpu.VMEM((parts, blocks, rows, piece), F32),
+            pltpu.VMEM((parts, lines, rows, piece), F32),
+            pltpu.VMEM((parts, lines * 2, rows, piece), BF16),
+            pltpu.VMEM((parts, lines * 2, rows, piece), BF16),
+            pltpu.VMEM((parts, lines, rows, piece), BF16),
+            pltpu.VMEM((parts, lines, rows, piece), BF16),
+            pltpu.VMEM((parts, lines, rows, piece), BF16),
+            pltpu.VMEM((parts, lines, rows, piece), BF16),
+            pltpu.VMEM((parts, lines, rows, piece), BF16),
+            pltpu.VMEM((parts, lines, rows, piece), BF16),
+            dma((6,)),
+            dma((2, 2, lines)),
+            dma((2, 2, lines)),
+            dma((2, lines)),
+            dma((2, lines)),
+            dma((2, lines * 2)),
+            dma((2, lines * 2)),
+            dma((2, parts)),
+            dma((2, parts)),
+            dma((parts, lines)),
+            dma((parts, lines)),
+            dma((parts, lines)),
+            dma((parts, lines)),
+        ],
+        compiler_params=pltpu.CompilerParams(
+            collective_id=0, has_side_effects=True, vmem_limit_bytes=48 * 2**20
+        ),
+        cost_estimate=pl.CostEstimate(
+            flops=14 * total * width * hidden,
+            bytes_accessed=6 * width * hidden + 10 * rows * width,
+            transcendentals=total * hidden,
+        ),
+    )(x, v, c, routes, rw, g, u, d)
 
 
 def route_terms(rows_x, rows_v, rows_c, rows_w, gate_w, up_w, down_w):
@@ -36,6 +392,10 @@
     tok_rows, width = tokens.shape
     top_count = routes.shape[1]
     slots = 2 * tok_rows * top_count // experts
+    if slots >= tok_rows and experts % 4 == 0 and experts <= LANES:
+        return whole_blocks(
+            tokens, tangent, cotangent, routes, route_weight, gate_weight, up_weight, down_weight
+        )
     routed = tok_rows * top_count
     flat_routes = routes.reshape(-1)
     onehot = (flat_routes[:, None] == jnp.arange(experts, dtype=jnp.int32)[None, :]).astype(

time: 160 us -> 61.4 us (0.38)
  blocking collectives: 60.9 us -> 0 us
  Pallas kernels: 0 us -> 54.5 us
  waiting for transfers between devices: 38.2 us -> 0 us
  starting transfers between devices: 19.3 us -> 0 us
  matrix products: 14.6 us -> 0 us
  local copies, waits for them, and re-layouts: 17.8 us -> 6.58 us
  other arithmetic: 7.01 us -> 0 us
    all_to_all x2 -> x0, blocking collectives: 60.9 us -> none  [the longest x1 31 us: shards(): lax.all_to_all(send_x, 'expert', split_axis=0, concat_axis=0, tiled=True)]
    pallas_call x0 -> x1, Pallas kernels: none -> 54.5 us  [whole_blocks(): pl.pallas_call(functools.partial(whole_block_kernel, lines, parts), out_s...]
    all_to_all x3 -> x0, waiting for transfers between devices: 38.2 us -> none  [the longest x1 23 us: shards(): lax.all_to_all(terms, 'expert', split_axis=0, concat_axis=0, tiled=True)]
    all_to_all x3 -> x0, starting transfers between devices: 19.3 us -> none  [the longest x1 7.39 us: shards(): lax.all_to_all(send_w, 'expert', split_axis=0, concat_axis=0, tiled=True)]
    dot_general x5 -> x0, matrix products: 14.6 us -> none  [the longest x1 4.65 us: route_terms(): gate_both = jnp.dot(stacked, gate_w, preferred_element_type=jnp.float32)]
    gather x5 -> x0, local copies, waits for them, and re-layouts: 12.5 us -> none  [the longest x3 7.04 us: place(): values[owner]]
    unnamed x22 -> x11, local copies, waits for them, and re-layouts: 2.1 us -> 6.58 us
    select_n x4 -> x0, other arithmetic: 3.65 us -> none  [the longest x1 3.63 us: place(): jnp.where(filled[:, None], values[owner], jnp.zeros((), values.dtype))]
  transfers between devices with their start and end apart: 3 -> 0, of which waited for: 2 -> 0; matrix products, arithmetic and copies ran while one was open for 12% -> 0% of each run, Pallas kernels for 0% -> 0%
where the time goes in v1:
time: 61.4 us; the launch traced here: 61.1 us
  Pallas kernels  54.5 us (89%)
  local copies, waits for them, and re-layouts  6.58 us (11%)
    pallas_call x1, Pallas kernels, whole_blocks(): pl.pallas_call(functools.partial(whole_block_kernel, lines, parts), out_s...  54.5 us
    unnamed x11, local copies, waits for them, and re-layouts  6.58 us

profile of v1, /device:TPU:0, one launch (start us, length us, event | category | flops | bytes accessed | tf_op | source)
XLA Modules:
  0.0 61.1 jit_solution(8267889480676554117)
XLA Ops:
  0.0 0.8 %copy.10.rw_ref = bf16[16,8]{1,0:T(8,128)(2,1)S(1)} copy(bf16[16,8]{0,1:T(8,128)(2,1)} %param.12) | data formatting | bytes 512 | tf_op args[4]
  0.8 0.8 %copy.9.routes_ref = s32[16,8]{1,0:T(8,128)S(1)} copy(s32[16,8]{0,1:T(8,128)} %param.11) | data formatting | bytes 1024 | tf_op args[3]
  1.5 0.0 copy-start
  1.5 1.9 %copy-done = bf16[1,2048,768]{2,1,0:T(8,128)(2,1)S(1)} copy-done((bf16[1,2048,768]{2,1,0:T(8,128)(2,1)S(1)}, bf16[1,2048,768]{2,1,0:T(8,128)(2,1)}, u32[]{:S(2)}) %copy-start) | copy-done | bytes 3145752
  3.4 0.0 copy-start.1
  3.4 0.8 %copy-done.1 = bf16[16,2048]{1,0:T(8,128)(2,1)S(1)} copy-done((bf16[16,2048]{1,0:T(8,128)(2,1)S(1)}, bf16[16,2048]{1,0:T(8,128)(2,1)}, u32[]{:S(2)}) %copy-start.1) | copy-done | bytes 65560
  4.2 0.0 copy-start.2
  4.2 0.8 %copy-done.2 = bf16[16,2048]{1,0:T(8,128)(2,1)S(1)} copy-done((bf16[16,2048]{1,0:T(8,128)(2,1)S(1)}, bf16[16,2048]{1,0:T(8,128)(2,1)}, u32[]{:S(2)}) %copy-start.2) | copy-done | bytes 65560
  5.1 0.0 copy-start.3
  5.1 0.8 %copy-done.3 = bf16[16,2048]{1,0:T(8,128)(2,1)S(1)} copy-done((bf16[16,2048]{1,0:T(8,128)(2,1)S(1)}, bf16[16,2048]{1,0:T(8,128)(2,1)}, u32[]{:S(2)}) %copy-start.3) | copy-done | bytes 65560
  5.9 54.5 %shard_map.82 = f32[16,2048]{1,0:T(8,128)S(1)} custom-call(bf16[16,2048]{1,0:T(8,128)(2,1)S(1)} %copy-done.1, bf16[16,2048]{1,0:T(8,128)(2,1)S(1)} %copy-done.2, bf16[16,2048]{1,0:T(8,128)(2,1)S(1)} %copy-done.3, s32[16,8]{1,0:T(8,128)S(1)} %copy.9.routes_ref, bf16[16,8]{1,0:T(8,128)(2,1)S(1)} %copy.10.rw_ref, bf16[1,2048,768]{2,1,0:T(8,128)(2,1)S(1)} %copy-done, ...), custom_call_target="tpu_custom_call" | custom-call | flops 5637144576 | bytes 9764864 | tf_op jit(solution)/shard_map/pallas_call | solution.py:313
  60.4 0.7 %copy.12 = f32[16,2048]{1,0:T(8,128)} copy(f32[16,2048]{1,0:T(8,128)S(1)} %shard_map.82) | data formatting | bytes 262144
Async XLA Ops:
  1.5 1.9 %copy-start = (bf16[1,2048,768]{2,1,0:T(8,128)(2,1)S(1)}, bf16[1,2048,768]{2,1,0:T(8,128)(2,1)}, u32[]{:S(2)}) copy-start(bf16[1,2048,768]{2,1,0:T(8,128)(2,1)} %g_hbm.1) | copy-start | bytes 9437188
  3.4 0.8 %copy-start.1 = (bf16[16,2048]{1,0:T(8,128)(2,1)S(1)}, bf16[16,2048]{1,0:T(8,128)(2,1)}, u32[]{:S(2)}) copy-start(bf16[16,2048]{1,0:T(8,128)(2,1)} %x_hbm.1) | copy-start | bytes 196612
  4.2 0.8 %copy-start.2 = (bf16[16,2048]{1,0:T(8,128)(2,1)S(1)}, bf16[16,2048]{1,0:T(8,128)(2,1)}, u32[]{:S(2)}) copy-start(bf16[16,2048]{1,0:T(8,128)(2,1)} %v_hbm.1) | copy-start | bytes 196612
  5.1 0.8 %copy-start.3 = (bf16[16,2048]{1,0:T(8,128)(2,1)S(1)}, bf16[16,2048]{1,0:T(8,128)(2,1)}, u32[]{:S(2)}) copy-start(bf16[16,2048]{1,0:T(8,128)(2,1)} %c_hbm.1) | copy-start | bytes 196612

commit v2 on v0

--- a/solution.py
+++ b/solution.py
@@ -1,7 +1,372 @@
 import jax
 import jax.numpy as jnp
 from jax import lax
+from jax.experimental import pallas as pl
+from jax.experimental.pallas import tpu as pltpu
 from jax.sharding import PartitionSpec as P
+
+LANES = 128
+LINES = 4
+BF16 = jnp.bfloat16
+F32 = jnp.float32
+NT = (((1,), (1,)), ((), ()))
+
+
+def whole_block_kernel(
+    x_hbm, v_hbm, c_hbm, routes_ref, rw_ref, g_hbm, u_hbm, d_hbm, out_ref,
+    xv, cw, g, u, d, a_s, b_s, gc, uc, term, q,
+    s1, r1, s2, r2, sq, rq,
+    local, zs, zr, ys, yr, ss, sr, sib_s, sib_r, col_s, col_r, line_s, line_r,
+):
+    rows, width = x_hbm.shape
+    hidden = g.shape[1]
+    lines = LINES
+    last = lines - 1
+    half = lines * 2 * rows
+    parts = term.shape[1]
+    piece = width // parts
+    me = lax.axis_index("expert")
+    core = lax.rem(me, 2)
+    y = lax.rem(lax.div(me, 2), 2)
+    z = lax.div(me, 4)
+    pair = lax.div(z, 2)
+    low = lax.rem(z, 2)
+    base = (2 * pair, 2 * (1 - pair))
+
+    def dev(zz, yy, cc):
+        return (zz * 2 + yy) * 2 + cc
+
+    sib = dev(z, y, 1 - core)
+    ynb = dev(z, 1 - y, core)
+
+    def remote(src, dst, send, recv, target):
+        return pltpu.make_async_remote_copy(
+            src_ref=src, dst_ref=dst, send_sem=send, recv_sem=recv,
+            device_id={"expert": target}, device_id_type=pl.DeviceIdType.MESH,
+        )
+
+    loads = [
+        pltpu.make_async_copy(x_hbm, xv.at[0, me], local.at[0]),
+        pltpu.make_async_copy(v_hbm, xv.at[1, me], local.at[1]),
+        pltpu.make_async_copy(c_hbm, cw.at[me, :, pl.ds(0, width)], local.at[2]),
+        pltpu.make_async_copy(g_hbm.at[0], g, local.at[3]),
+        pltpu.make_async_copy(u_hbm.at[0], u, local.at[4]),
+        pltpu.make_async_copy(d_hbm.at[0], d, local.at[5]),
+    ]
+    for load in loads:
+        load.start()
+
+    barrier = pltpu.get_barrier_semaphore()
+    peers = [sib, ynb] + [dev(lax.rem(z + o, lines), y, core) for o in range(1, lines)]
+    for peer in peers:
+        pl.semaphore_signal(
+            barrier, inc=1, device_id={"expert": peer}, device_id_type=pl.DeviceIdType.MESH
+        )
+
+    lane = lax.broadcasted_iota(jnp.int32, (rows, LANES), 1)
+    eye = lax.broadcasted_iota(jnp.int32, (rows, rows), 0) == lax.broadcasted_iota(
+        jnp.int32, (rows, rows), 1
+    )
+    routes = routes_ref[...].astype(F32)
+    weights = rw_ref[...].astype(F32)
+    table = jnp.zeros((rows, LANES), F32)
+    for k in range(routes.shape[0]):
+        route = jnp.sum(jnp.where(eye, routes[k : k + 1, :], 0.0), axis=1, keepdims=True)
+        weight = jnp.sum(jnp.where(eye, weights[k : k + 1, :], 0.0), axis=1, keepdims=True)
+        table = table + jnp.where(route.astype(jnp.int32) == lane, weight, 0.0)
+    cw[me, :, width:] = table.astype(BF16)
+
+    pl.semaphore_wait(barrier, len(peers))
+
+    def block(p, index):
+        return cw.at[index] if p == 2 else xv.at[p, index]
+
+    def zcopy(p, way, s, reach=1):
+        ref = block(p, dev(s, y, core))
+        step = 4 * reach
+        target = me + step if way == 0 else me - step
+        return remote(ref, ref, zs.at[p, way, s, reach // 2], zr.at[p, way, s], target)
+
+    def ycopy(p, s, col):
+        ref = block(p, dev(s, col, core))
+        return remote(ref, ref, ys.at[p, s], yr.at[p, s], ynb)
+
+    def scopy(p, k, plane):
+        ref = block(p, k * 2 + plane)
+        return remote(ref, ref, ss.at[p, k], sr.at[p, k], sib)
+
+    def own(p, go):
+        @pl.when(z < last)
+        def _():
+            go(zcopy(p, 0, z))
+
+        @pl.when(z > 0)
+        def _():
+            go(zcopy(p, 1, z))
+
+        go(ycopy(p, z, y))
+
+        @pl.when(z == 0)
+        def _():
+            go(zcopy(p, 0, z, last))
+
+        @pl.when(z == last)
+        def _():
+            go(zcopy(p, 1, z, last))
+
+        go(scopy(p, z * 2 + y, core))
+
+    def near(t, fn):
+        @pl.when(z >= t)
+        def _():
+            fn(0, z - t)
+
+        @pl.when(z + t <= last)
+        def _():
+            fn(1, z + t)
+
+    def forward(p, t, way, s, go):
+        if t == 1:
+            @pl.when(z < last if way == 0 else z > 0)
+            def _():
+                go(zcopy(p, way, s))
+        go(ycopy(p, s, y))
+        go(scopy(p, s * 2 + y, core))
+
+    def hop(p, t):
+        def arrive(way, s):
+            zcopy(p, way, s).wait_recv()
+            forward(p, t, way, s, lambda copy: copy.start())
+        near(t, arrive)
+
+    def across(p, t):
+        def arrive(way, s):
+            ycopy(p, s, 1 - y).wait_recv()
+            scopy(p, s * 2 + 1 - y, core).start()
+        if t == 0:
+            arrive(0, z)
+        else:
+            near(t, arrive)
+
+    def from_sibling(p, h):
+        for k in range(4):
+            scopy(p, 2 * base[h] + k, 1 - core).wait_recv()
+
+    tile = 256
+    tiles = hidden // tile
+
+    def both(h, n):
+        cols = slice(n * tile, (n + 1) * tile)
+        stacked = xv[:, pl.ds(4 * base[h], 8)].reshape(2 * half, width)
+        gate_both = jnp.dot(stacked, g[:, cols], preferred_element_type=F32)
+        up_both = jnp.dot(stacked, u[:, cols], preferred_element_type=F32)
+        gate, gate_dot = gate_both[:half], gate_both[half:]
+        upper, up_dot = up_both[:half], up_both[half:]
+        sigma = jax.nn.sigmoid(gate)
+        first = sigma * (1.0 + gate * (1.0 - sigma))
+        second = sigma * (1.0 - sigma) * (2.0 + gate * (1.0 - 2.0 * sigma))
+        a_s[h, :, cols] = up_dot * first + upper * second * gate_dot
+        b_s[h, :, cols] = first * gate_dot
+
+    def changes(h):
+        rows_c = cw[pl.ds(4 * base[h], 8)].reshape(half, width + LANES)
+        tags = rows_c[:, width:].astype(F32)
+        mine = lax.broadcasted_iota(jnp.int32, (half, LANES), 1) == me
+        scale = jnp.sum(jnp.where(mine, tags, 0.0), axis=1, keepdims=True)
+        for n in range(tiles):
+            cols = slice(n * tile, (n + 1) * tile)
+            back = lax.dot_general(
+                rows_c[:, :width], d[cols, :], NT, preferred_element_type=F32
+            )
+            back = back * scale
+            gc[h, :, cols] = (back * a_s[h, :, cols]).astype(BF16)
+            uc[h, :, cols] = (back * b_s[h, :, cols]).astype(BF16)
+
+    def to_sibling(h, j):
+        return remote(s1.at[h, j], r1.at[h, j], sib_s.at[h, j], sib_r.at[h, j], sib)
+
+    def to_column(h, j):
+        return remote(s2.at[h, j], r2.at[h, j], col_s.at[h, j], col_r.at[h, j], ynb)
+
+    def to_line(h, j, l):
+        return remote(
+            sq.at[h, j, l], rq.at[j, z], line_s.at[h, j, l], line_r.at[j, z],
+            dev(base[h] + l, y, core),
+        )
+
+    def from_line(j, src):
+        return remote(sq.at[1, j, 0], rq.at[j, src], line_s.at[1, j, 0], line_r.at[j, src], sib)
+
+    def make_terms(h, j):
+        cols = slice(j * piece, (j + 1) * piece)
+        t = lax.dot_general(gc[h], g[cols, :], NT, preferred_element_type=F32)
+        t = t + lax.dot_general(uc[h], u[cols, :], NT, preferred_element_type=F32)
+        term[h, j] = t.reshape(8, rows, piece)
+        for k in range(4):
+            s1[h, j, k] = term[h, j, 2 * k + 1 - core].astype(BF16)
+        to_sibling(h, j).start()
+
+    def add_sibling(h, j):
+        to_sibling(h, j).wait_recv()
+        for l in range(2):
+            s2[h, j, l] = (
+                term[h, j, dev(l, 1 - y, core)] + r1[h, j, l * 2 + 1 - y].astype(F32)
+            ).astype(BF16)
+        to_column(h, j).start()
+        for l in range(2):
+            q[h, j, l] = term[h, j, dev(l, y, core)] + r1[h, j, l * 2 + y].astype(F32)
+
+    def add_column(h, j):
+        to_column(h, j).wait_recv()
+        if h == 1:
+            for l in range(2):
+                sq[h, j, l] = (q[h, j, l] + r2[h, j, l].astype(F32)).astype(BF16)
+                to_line(h, j, l).start()
+        else:
+            other = 1 - low
+            sq[h, j, other] = (q[h, j, other] + r2[h, j, other].astype(F32)).astype(BF16)
+            to_line(h, j, other).start()
+            cols = slice(j * piece, (j + 1) * piece)
+            out_ref[:, cols] = q[h, j, low] + r2[h, j, low].astype(F32)
+
+    loads[0].wait()
+    own(0, lambda copy: copy.start())
+    loads[1].wait()
+    own(1, lambda copy: copy.start())
+    loads[2].wait()
+    hop(0, 1)
+    hop(1, 1)
+    own(2, lambda copy: copy.start())
+    across(0, 0)
+    across(1, 0)
+    hop(0, 2)
+    hop(1, 2)
+    hop(2, 1)
+    across(0, 1)
+    across(1, 1)
+    across(2, 0)
+    for load in loads[3:]:
+        load.wait()
+    from_sibling(0, 0)
+    from_sibling(1, 0)
+    hop(0, 3)
+    hop(1, 3)
+    both(0, 0)
+    hop(2, 2)
+    hop(2, 3)
+    across(0, 2)
+    across(1, 2)
+    for n in range(1, tiles):
+        both(0, n)
+        across(n - 1, 3)
+    across(2, 1)
+    from_sibling(2, 0)
+    changes(0)
+    from_sibling(0, 1)
+    from_sibling(1, 1)
+    for n in range(tiles):
+        both(1, n)
+    across(2, 2)
+    across(2, 3)
+    for j in range(parts):
+        make_terms(0, j)
+    for j in range(parts):
+        add_sibling(0, j)
+    from_sibling(2, 1)
+    changes(1)
+    for j in range(parts):
+        make_terms(1, j)
+        if j > 0:
+            add_sibling(1, j - 1)
+    add_sibling(1, parts - 1)
+    for j in range(parts):
+        add_column(0, j)
+    for j in range(parts):
+        add_column(1, j)
+    for j in range(parts):
+        cols = slice(j * piece, (j + 1) * piece)
+        sources = (base[0] + 1 - low, base[1], base[1] + 1)
+        for src in sources:
+            from_line(j, src).wait_recv()
+        out_ref[:, cols] += (
+            rq[j, sources[0]].astype(F32)
+            + rq[j, sources[1]].astype(F32)
+            + rq[j, sources[2]].astype(F32)
+        )
+
+    for p in range(3):
+        own(p, lambda copy: copy.wait_send())
+        scopy(p, z * 2 + 1 - y, core).wait_send()
+        for t in range(1, lines):
+            def gone(way, s):
+                forward(p, t, way, s, lambda copy: copy.wait_send())
+                scopy(p, s * 2 + 1 - y, core).wait_send()
+            near(t, gone)
+    for j in range(parts):
+        for h in range(2):
+            to_sibling(h, j).wait_send()
+            to_column(h, j).wait_send()
+        to_line(0, j, 1 - low).wait_send()
+        to_line(1, j, 0).wait_send()
+        to_line(1, j, 1).wait_send()
+
+
+def whole_blocks(x, v, c, routes, rw, g, u, d):
+    rows, width = x.shape
+    hidden = g.shape[2]
+    blocks = LINES * 4
+    half = blocks * rows // 2
+    parts = 2
+    piece = width // parts
+    dma = pltpu.SemaphoreType.DMA
+    hbm = pl.BlockSpec(memory_space=pltpu.HBM)
+    vmem = pl.BlockSpec(memory_space=pltpu.VMEM)
+    return pl.pallas_call(
+        whole_block_kernel,
+        out_shape=jax.ShapeDtypeStruct((rows, width), F32),
+        in_specs=[hbm] * 3 + [vmem] * 2 + [hbm] * 3,
+        out_specs=vmem,
+        scratch_shapes=[
+            pltpu.VMEM((2, blocks, rows, width), BF16),
+            pltpu.VMEM((blocks, rows, width + LANES), BF16),
+            pltpu.VMEM((width, hidden), BF16),
+            pltpu.VMEM((width, hidden), BF16),
+            pltpu.VMEM((hidden, width), BF16),
+            pltpu.VMEM((2, half, hidden), F32),
+            pltpu.VMEM((2, half, hidden), F32),
+            pltpu.VMEM((2, half, hidden), BF16),
+            pltpu.VMEM((2, half, hidden), BF16),
+            pltpu.VMEM((2, parts, blocks // 2, rows, piece), F32),
+            pltpu.VMEM((2, parts, 2, rows, piece), F32),
+            pltpu.VMEM((2, parts, 4, rows, piece), BF16),
+            pltpu.VMEM((2, parts, 4, rows, piece), BF16),
+            pltpu.VMEM((2, parts, 2, rows, piece), BF16),
+            pltpu.VMEM((2, parts, 2, rows, piece), BF16),
+            pltpu.VMEM((2, parts, 2, rows, piece), BF16),
+            pltpu.VMEM((parts, LINES, rows, piece), BF16),
+            dma((6,)),
+            dma((3, 2, LINES, 2)),
+            dma((3, 2, LINES)),
+            dma((3, LINES)),
+            dma((3, LINES)),
+            dma((3, LINES * 2)),
+            dma((3, LINES * 2)),
+            dma((2, parts)),
+            dma((2, parts)),
+            dma((2, parts)),
+            dma((2, parts)),
+            dma((2, parts, 2)),
+            dma((parts, LINES)),
+        ],
+        compiler_params=pltpu.CompilerParams(
+            collective_id=0, has_side_effects=True, vmem_limit_bytes=56 * 2**20
+        ),
+        cost_estimate=pl.CostEstimate(
+            flops=28 * half * width * hidden,
+            bytes_accessed=6 * width * hidden + 10 * rows * width,
+            transcendentals=2 * half * hidden,
+        ),
+    )(x, v, c, routes.T, rw.T, g, u, d)
 
 
 def route_terms(rows_x, rows_v, rows_c, rows_w, gate_w, up_w, down_w):
@@ -36,6 +401,10 @@
     tok_rows, width = tokens.shape
     top_count = routes.shape[1]
     slots = 2 * tok_rows * top_count // experts
+    if slots >= tok_rows and experts == 4 * LINES:
+        return whole_blocks(
+            tokens, tangent, cotangent, routes, route_weight, gate_weight, up_weight, down_weight
+        )
     routed = tok_rows * top_count
     flat_routes = routes.reshape(-1)
     onehot = (flat_routes[:, None] == jnp.arange(experts, dtype=jnp.int32)[None, :]).astype(

time: 160 us -> 50.5 us (0.32); the launches traced: 158 us -> 50.3 us
  blocking collectives: 60.9 us -> 0 us
  Pallas kernels: 0 us -> 48.7 us
  waiting for transfers between devices: 38.2 us -> 0 us
  starting transfers between devices: 19.3 us -> 0 us
  local copies, waits for them, and re-layouts: 17.8 us -> 1.57 us
  matrix products: 14.6 us -> 0 us
  other arithmetic: 7.01 us -> 0 us
    all_to_all x2 -> x0, blocking collectives: 60.9 us -> none  [the longest x1 31 us: shards(): lax.all_to_all(send_x, 'expert', split_axis=0, concat_axis=0, tiled=True)]
    pallas_call x0 -> x1, Pallas kernels: none -> 48.7 us  [whole_blocks(): pl.pallas_call(whole_block_kernel, out_shape=jax.ShapeDtypeStruct((rows,...]
    all_to_all x3 -> x0, waiting for transfers between devices: 38.2 us -> none  [the longest x1 23 us: shards(): lax.all_to_all(terms, 'expert', split_axis=0, concat_axis=0, tiled=True)]
    all_to_all x3 -> x0, starting transfers between devices: 19.3 us -> none  [the longest x1 7.39 us: shards(): lax.all_to_all(send_w, 'expert', split_axis=0, concat_axis=0, tiled=True)]
    dot_general x5 -> x0, matrix products: 14.6 us -> none  [the longest x1 4.65 us: route_terms(): gate_both = jnp.dot(stacked, gate_w, preferred_element_type=jnp.float32)]
    gather x5 -> x0, local copies, waits for them, and re-layouts: 12.5 us -> none  [the longest x3 7.04 us: place(): values[owner]]
    select_n x4 -> x0, other arithmetic: 3.65 us -> none  [the longest x1 3.63 us: place(): jnp.where(filled[:, None], values[owner], jnp.zeros((), values.dtype))]
    reduce_sum x2 -> x0, other arithmetic: 2.21 us -> none  [the longest x1 2.04 us: shards(): return jnp.sum(per_route, axis=1)]
  transfers between devices with their start and end apart: 3 -> 0, of which waited for: 2 -> 0; matrix products, arithmetic and copies ran while one was open for 12% -> 0% of each run, Pallas kernels for 0% -> 0%
where the time goes in v2:
time: 50.5 us; the launch traced here: 50.3 us
  Pallas kernels  48.7 us (96%)
  local copies, waits for them, and re-layouts  1.57 us (3%)
    pallas_call x1, Pallas kernels, whole_blocks(): pl.pallas_call(whole_block_kernel, out_shape=jax.ShapeDtypeStruct((rows,...  48.7 us
    unnamed x1, local copies, waits for them, and re-layouts  1.57 us

profile of v2, /device:TPU:0, one launch (start us, length us, event | category | flops | bytes accessed | tf_op | source)
XLA Modules:
  0.0 50.3 jit_solution(2492183605868343021)
XLA Ops:
  0.0 48.7 %shard_map.82 = f32[16,2048]{1,0:T(8,128)} custom-call(bf16[16,2048]{1,0:T(8,128)(2,1)} %x_hbm.1, bf16[16,2048]{1,0:T(8,128)(2,1)} %v_hbm.1, bf16[16,2048]{1,0:T(8,128)(2,1)} %c_hbm.1, s32[8,16]{1,0:T(8,128)} %bitcast.2, bf16[8,16]{1,0:T(8,128)(2,1)} %bitcast.3, bf16[1,2048,768]{2,1,0:T(8,128)(2,1)} %g_hbm.1, bf16[1,2048,768]{2,1,0:T(8,128)(2,1)} %u_hbm.1, ...), custom_call_target="tpu_custom_call" | custom-call | flops 5637144576 | bytes 9764864 | tf_op jit(solution)/shard_map/pallas_call | solution.py:324
  48.7 1.6 %copy.10 = f32[16,2048]{1,0:T(8,128)} copy(f32[16,2048]{1,0:T(8,128)} %shard_map.82) | data formatting | bytes 262144

commit v3 on v2

--- a/solution.py
+++ b/solution.py
@@ -57,11 +57,22 @@
         load.start()
 
     barrier = pltpu.get_barrier_semaphore()
-    peers = [sib, ynb] + [dev(lax.rem(z + o, lines), y, core) for o in range(1, lines)]
-    for peer in peers:
+
+    def greet(target):
         pl.semaphore_signal(
-            barrier, inc=1, device_id={"expert": peer}, device_id_type=pl.DeviceIdType.MESH
+            barrier, inc=1, device_id={"expert": target}, device_id_type=pl.DeviceIdType.MESH
         )
+
+    greet(sib)
+    greet(ynb)
+
+    @pl.when(z > 0)
+    def _():
+        greet(me - 4)
+
+    @pl.when(z < last)
+    def _():
+        greet(me + 4)
 
     lane = lax.broadcasted_iota(jnp.int32, (rows, LANES), 1)
     eye = lax.broadcasted_iota(jnp.int32, (rows, rows), 0) == lax.broadcasted_iota(
@@ -76,16 +87,15 @@
         table = table + jnp.where(route.astype(jnp.int32) == lane, weight, 0.0)
     cw[me, :, width:] = table.astype(BF16)
 
-    pl.semaphore_wait(barrier, len(peers))
+    pl.semaphore_wait(barrier, 2 + (z > 0).astype(jnp.int32) + (z < last).astype(jnp.int32))
 
     def block(p, index):
         return cw.at[index] if p == 2 else xv.at[p, index]
 
-    def zcopy(p, way, s, reach=1):
+    def zcopy(p, way, s):
         ref = block(p, dev(s, y, core))
-        step = 4 * reach
-        target = me + step if way == 0 else me - step
-        return remote(ref, ref, zs.at[p, way, s, reach // 2], zr.at[p, way, s], target)
+        target = me + 4 if way == 0 else me - 4
+        return remote(ref, ref, zs.at[p, way, s], zr.at[p, way, s], target)
 
     def ycopy(p, s, col):
         ref = block(p, dev(s, col, core))
@@ -106,14 +116,6 @@
 
         go(ycopy(p, z, y))
 
-        @pl.when(z == 0)
-        def _():
-            go(zcopy(p, 0, z, last))
-
-        @pl.when(z == last)
-        def _():
-            go(zcopy(p, 1, z, last))
-
         go(scopy(p, z * 2 + y, core))
 
     def near(t, fn):
@@ -126,10 +128,10 @@
             fn(1, z + t)
 
     def forward(p, t, way, s, go):
-        if t == 1:
-            @pl.when(z < last if way == 0 else z > 0)
-            def _():
-                go(zcopy(p, way, s))
+        @pl.when(z < last if way == 0 else z > 0)
+        def _():
+            go(zcopy(p, way, s))
+
         go(ycopy(p, s, y))
         go(scopy(p, s * 2 + y, core))
 
@@ -244,34 +246,36 @@
     hop(2, 1)
     across(0, 1)
     across(1, 1)
-    across(2, 0)
     for load in loads[3:]:
         load.wait()
     from_sibling(0, 0)
     from_sibling(1, 0)
+    both(0, 0)
     hop(0, 3)
+    both(0, 1)
     hop(1, 3)
-    both(0, 0)
     hop(2, 2)
-    hop(2, 3)
+    across(2, 0)
     across(0, 2)
+    both(0, 2)
     across(1, 2)
-    for n in range(1, tiles):
-        both(0, n)
-        across(n - 1, 3)
     across(2, 1)
     from_sibling(2, 0)
     changes(0)
+    across(0, 3)
+    hop(2, 3)
+    for j in range(parts):
+        make_terms(0, j)
+    across(1, 3)
     from_sibling(0, 1)
     from_sibling(1, 1)
-    for n in range(tiles):
-        both(1, n)
+    both(1, 0)
+    for j in range(parts):
+        add_sibling(0, j)
+    both(1, 1)
     across(2, 2)
+    both(1, 2)
     across(2, 3)
-    for j in range(parts):
-        make_terms(0, j)
-    for j in range(parts):
-        add_sibling(0, j)
     from_sibling(2, 1)
     changes(1)
     for j in range(parts):
@@ -345,7 +349,7 @@
             pltpu.VMEM((2, parts, 2, rows, piece), BF16),
             pltpu.VMEM((parts, LINES, rows, piece), BF16),
             dma((6,)),
-            dma((3, 2, LINES, 2)),
+            dma((3, 2, LINES)),
             dma((3, 2, LINES)),
             dma((3, LINES)),
             dma((3, LINES)),

time: 50.5 us -> 48.1 us (0.952)
  Pallas kernels: 48.7 us -> 46.3 us
    pallas_call x1, Pallas kernels: 48.7 us -> 46.3 us  [whole_blocks(): pl.pallas_call(whole_block_kernel, out_shape=jax.ShapeDtypeStruct((rows,...]
where the time goes in v3:
time: 48.1 us; the launch traced here: 47.9 us
  Pallas kernels  46.3 us (96%)
  local copies, waits for them, and re-layouts  1.57 us (3%)
    pallas_call x1, Pallas kernels, whole_blocks(): pl.pallas_call(whole_block_kernel, out_shape=jax.ShapeDtypeStruct((rows,...  46.3 us
    unnamed x1, local copies, waits for them, and re-layouts  1.57 us

profile of v3, /device:TPU:0, one launch (start us, length us, event | category | flops | bytes accessed | tf_op | source)
XLA Modules:
  0.0 47.9 jit_solution(9964496411762823313)
XLA Ops:
  0.0 46.3 %shard_map.82 = f32[16,2048]{1,0:T(8,128)} custom-call(bf16[16,2048]{1,0:T(8,128)(2,1)} %x_hbm.1, bf16[16,2048]{1,0:T(8,128)(2,1)} %v_hbm.1, bf16[16,2048]{1,0:T(8,128)(2,1)} %c_hbm.1, s32[8,16]{1,0:T(8,128)} %bitcast.2, bf16[8,16]{1,0:T(8,128)(2,1)} %bitcast.3, bf16[1,2048,768]{2,1,0:T(8,128)(2,1)} %g_hbm.1, bf16[1,2048,768]{2,1,0:T(8,128)(2,1)} %u_hbm.1, ...), custom_call_target="tpu_custom_call" | custom-call | flops 5637144576 | bytes 9764864 | tf_op jit(solution)/shard_map/pallas_call | solution.py:328
  46.3 1.6 %copy.10 = f32[16,2048]{1,0:T(8,128)} copy(f32[16,2048]{1,0:T(8,128)} %shard_map.82) | data formatting | bytes 262144

commit v4 on v3

--- a/solution.py
+++ b/solution.py
@@ -74,19 +74,6 @@
     def _():
         greet(me + 4)
 
-    lane = lax.broadcasted_iota(jnp.int32, (rows, LANES), 1)
-    eye = lax.broadcasted_iota(jnp.int32, (rows, rows), 0) == lax.broadcasted_iota(
-        jnp.int32, (rows, rows), 1
-    )
-    routes = routes_ref[...].astype(F32)
-    weights = rw_ref[...].astype(F32)
-    table = jnp.zeros((rows, LANES), F32)
-    for k in range(routes.shape[0]):
-        route = jnp.sum(jnp.where(eye, routes[k : k + 1, :], 0.0), axis=1, keepdims=True)
-        weight = jnp.sum(jnp.where(eye, weights[k : k + 1, :], 0.0), axis=1, keepdims=True)
-        table = table + jnp.where(route.astype(jnp.int32) == lane, weight, 0.0)
-    cw[me, :, width:] = table.astype(BF16)
-
     pl.semaphore_wait(barrier, 2 + (z > 0).astype(jnp.int32) + (z < last).astype(jnp.int32))
 
     def block(p, index):
@@ -235,6 +222,19 @@
     own(0, lambda copy: copy.start())
     loads[1].wait()
     own(1, lambda copy: copy.start())
+    lane = lax.broadcasted_iota(jnp.int32, (rows, LANES), 1)
+    eye = lax.broadcasted_iota(jnp.int32, (rows, rows), 0) == lax.broadcasted_iota(
+        jnp.int32, (rows, rows), 1
+    )
+    routes = routes_ref[...].astype(F32)
+    weights = rw_ref[...].astype(F32)
+    table = jnp.zeros((rows, LANES), F32)
+    for k in range(routes.shape[0]):
+        route = jnp.sum(jnp.where(eye, routes[k : k + 1, :], 0.0), axis=1, keepdims=True)
+        weight = jnp.sum(jnp.where(eye, weights[k : k + 1, :], 0.0), axis=1, keepdims=True)
+        table = table + jnp.where(route.astype(jnp.int32) == lane, weight, 0.0)
+    cw[me, :, width:] = table.astype(BF16)
+
     loads[2].wait()
     hop(0, 1)
     hop(1, 1)

time: 48.1 us -> 48.1 us (level)
  no operation moved by 1% of the time
where the time goes in v4:
time: 48.1 us; the launch traced here: 47.9 us
  Pallas kernels  46.3 us (96%)
  local copies, waits for them, and re-layouts  1.57 us (3%)
    pallas_call x1, Pallas kernels, whole_blocks(): pl.pallas_call(whole_block_kernel, out_shape=jax.ShapeDtypeStruct((rows,...  46.3 us
    unnamed x1, local copies, waits for them, and re-layouts  1.57 us

profile of v4, /device:TPU:0, one launch (start us, length us, event | category | flops | bytes accessed | tf_op | source)
XLA Modules:
  0.0 47.9 jit_solution(2999338549398535161)
XLA Ops:
  0.0 46.3 %shard_map.82 = f32[16,2048]{1,0:T(8,128)} custom-call(bf16[16,2048]{1,0:T(8,128)(2,1)} %x_hbm.1, bf16[16,2048]{1,0:T(8,128)(2,1)} %v_hbm.1, bf16[16,2048]{1,0:T(8,128)(2,1)} %c_hbm.1, s32[8,16]{1,0:T(8,128)} %bitcast.2, bf16[8,16]{1,0:T(8,128)(2,1)} %bitcast.3, bf16[1,2048,768]{2,1,0:T(8,128)(2,1)} %g_hbm.1, bf16[1,2048,768]{2,1,0:T(8,128)(2,1)} %u_hbm.1, ...), custom_call_target="tpu_custom_call" | custom-call | flops 5637144576 | bytes 9764864 | tf_op jit(solution)/shard_map/pallas_call | solution.py:328
  46.3 1.6 %copy.10 = f32[16,2048]{1,0:T(8,128)} copy(f32[16,2048]{1,0:T(8,128)} %shard_map.82) | data formatting | bytes 262144
